TPU v7x, 128 devices: a whole 4x4x4 slice. The times are simulated.
128 devices in a mesh: views: 4 (over z_hi, core), slab: 32 (over z_lo, y, x).
Axes of the slice: x: 4, y: 4, z: 4 (z_hi: 2, z_lo: 2; z = z_hi * 2 + z_lo), core: 2. Of those that a mesh axis runs over, the one named last changes fastest.
Arguments:
- tiles: bfloat16 [2, 32, 640, 16, 256], P(None, 'slab', 'views'), may hold values from 0 to 0.25
- lor_weight: bfloat16 [2, 32, 640, 16], P(None, 'slab', 'views'), may hold values from 0.049804688 to 1
- block_map: int32 [2, 32, 640], P(None, 'slab', 'views'), may hold values from 0 to 2699
- kernel_weight: bfloat16 [147, 32, 230400], P(None, 'slab', 'views'), may hold values from 0 to 0.04, as said below
Outputs:
- sensitivity: float32 [32, 230400], P('slab', 'views')
Inputs may be any that keep to these rules, and one draw needn't show every extreme that they name: `kernel_weight`: for each voxel exactly 50 of its 147 box entries are nonzero (its kernel neighbours); the others are zero.
All inputs are finite; a program needn't handle non-finite values.
Results may differ from a plain program's by a relative error of at most 0.0003.
Values sent between devices are 32-bit elements; how exact they have to be, the bound alone decides.
A program may use at most 384 MiB of HBM per device.

v0:
```python
import functools

import jax
import jax.numpy as jnp
from jax import lax
from jax.experimental import pallas as pl
from jax.experimental.pallas import tpu as pltpu
from jax.sharding import PartitionSpec as P

MESH = pl.DeviceIdType.MESH
NCOL = 480
LANES = 128
BLOCK = 256
HALO = 6
BANDED = 240
ROWS = 2 * BANDED
LEAD = HALO * BLOCK - 3 * NCOL
QUAD = 4 * NCOL // LANES
PARTS = 4
MARKS = (0, 128, 248, 368, ROWS)
CHUNKS = len(MARKS) - 1
BOX_MARKS = (0, 3, 7, 11, 15)
PIECES = 4
AHEAD = 2
RING = 8


def kernel(
    plane_blocks, tiles_hbm, lor_ref, map_ref, kw_hbm, out_ref,
    tiles, raw, weights, contrib, keys, band, zsend, zrecv, plane, shifted, result,
    tile_sem, raw_sem, raw_send, raw_recv, sib_send, sib_recv, fwd_send, fwd_recv, key_send, key_recv,
    z_send, z_recv, x_send, x_recv,
):
    subsets, lors, per_dev = lor_ref.shape
    entries, voxels = kw_hbm.shape
    count = subsets * per_dev
    piece = count // PIECES
    band_blocks = voxels // BLOCK
    quads = voxels // (QUAD * LANES)

    v = lax.axis_index("views")
    s = lax.axis_index("slab")
    slabs = lax.axis_size("slab")
    sibling = (v // 2 * 2 + 1 - lax.rem(v, 2), s)
    opposite = lax.rem(v + 2, 4)
    across = (opposite, s)
    above = (v, lax.rem(s + 1, slabs))
    below = (v, lax.rem(s + slabs - 1, slabs))

    barrier = pltpu.get_barrier_semaphore()
    for device in (sibling, across, above, below):
        pl.semaphore_signal(barrier, inc=1, device_id=device, device_id_type=MESH)

    def remote(src, dst, send, recv, device):
        return pltpu.make_async_remote_copy(
            src_ref=src, dst_ref=dst, send_sem=send, recv_sem=recv, device_id=device, device_id_type=MESH
        )

    piece_rows = piece * lors
    tile_loads = [
        pltpu.make_async_copy(
            tiles_hbm.at[pl.ds(n * piece_rows, piece_rows)], tiles.at[pl.ds(n * piece_rows, piece_rows)], tile_sem.at[n]
        )
        for n in range(PIECES)
    ]
    for load in tile_loads:
        load.start()

    def raw_load(m, slot):
        lanes = QUAD * LANES
        start = m * lanes if isinstance(m, int) else pl.multiple_of(m * lanes, lanes)
        return pltpu.make_async_copy(kw_hbm.at[:, pl.ds(start, lanes)], raw.at[slot], raw_sem.at[slot])

    for m in range(RING):
        raw_load(m, m).start()

    to_x, to_fwd, key_copies = [], [], []
    for n in range(PIECES):
        rows = pl.ds(n * piece, piece)
        pair = []
        for side, (target, device) in enumerate(((1, above), (2, below))):
            pair.append(
                remote(contrib.at[0, rows], contrib.at[target, rows], raw_send.at[side, n], raw_recv.at[side, n], device)
            )
        to_x.append(pair)
        to_fwd.append(
            [
                remote(
                    contrib.at[side + 1, rows], contrib.at[side + 4, rows],
                    fwd_send.at[side, n], fwd_recv.at[side, n], sibling,
                )
                for side in range(2)
            ]
        )
    for n, (source, target, device) in enumerate(
        ((0, 1, above), (0, 2, below), (0, 3, sibling), (1, 4, sibling), (2, 5, sibling))
    ):
        key_copies.append(remote(keys.at[source], keys.at[target], key_send.at[n], key_recv.at[n], device))
    to_sibling = remote(contrib.at[0], contrib.at[3], sib_send.at[0], sib_recv.at[0], sibling)

    width = keys.shape[2]
    pad = jnp.full((1, width - count), -1, jnp.int32)
    row = jnp.concatenate([map_ref[u] for u in range(subsets)] + [pad], axis=1)
    keys[0] = jnp.broadcast_to(row, keys.shape[1:])
    spread = (
        lax.rem(lax.broadcasted_iota(jnp.int32, (lors, BLOCK), 1), lors)
        == lax.broadcasted_iota(jnp.int32, (lors, BLOCK), 0)
    ).astype(jnp.float32).astype(jnp.bfloat16)
    group = BLOCK // lors
    diagonal = (
        lax.rem(lax.broadcasted_iota(jnp.int32, (per_dev, BLOCK), 0), group)
        == lax.broadcasted_iota(jnp.int32, (per_dev, BLOCK), 1) // lors
    )
    wide = []
    for u in range(subsets):
        spread_out = lax.dot_general(
            lor_ref[u], spread, (((0,), (0,)), ((), ())), preferred_element_type=jnp.float32
        )
        wide.append(jnp.where(diagonal, spread_out, 0.0).astype(jnp.bfloat16))
    for n in range(PIECES):
        tile_loads[n].wait()
        for first in range(n * piece, (n + 1) * piece, group):
            own = first % per_dev
            contrib[0, pl.ds(first, group), :] = jnp.dot(
                wide[first // per_dev][own : own + group], tiles[pl.ds(first * lors, BLOCK), :],
                preferred_element_type=jnp.float32,
            )
        if n == 0:
            pl.semaphore_wait(barrier, 4)
            for k in range(3):
                key_copies[k].start()
        if n < AHEAD:
            for copy in to_x[n]:
                copy.start()
    to_sibling.start()

    lane16 = lax.broadcasted_iota(jnp.int32, (16, LANES), 1)

    def turn(slot, m):
        for base in range(0, entries, 16):
            size = min(16, entries - base)
            here = [raw[slot, pl.ds(base, size), pl.ds(c * LANES, LANES)] for c in range(QUAD)]
            for i in range(4):
                first, a = divmod(NCOL * i, LANES)
                for q in range(PARTS):
                    values = here[first + q]
                    if a:
                        if first + q + 1 < QUAD:
                            values = jnp.where(lane16[0:size] >= a, values, here[first + q + 1])
                        values = pltpu.roll(values, LANES - a, 1)
                    values = values.astype(jnp.float32)
                    for half in range(0, size, 8):
                        some = min(8, size - half)
                        weights[(base + half) // 8 * PARTS + q, pl.ds((4 * m + i) * 8, some), :] = values[
                            half : half + some
                        ]

    def turn_quads(low, high):
        @pl.loop(low, high)
        def _(m):
            slot = lax.rem(m, RING)
            raw_load(m, slot).wait()
            turn(slot, m)

            @pl.when(m + RING < quads)
            def _():
                raw_load(m + RING, slot).start()

    def scatter(sets, into, first):
        for index in sets:
            delta = (0, -1, 1)[index % 3]
            whole = contrib[index]
            high = whole.astype(jnp.bfloat16)
            low = (whole - high.astype(jnp.float32)).astype(jnp.bfloat16)
            place = keys[index][0:1, 0:count] - plane_blocks * (1 - delta)
            if delta < 0:
                place = jnp.where(s > 0, place, -1)
            if delta > 0:
                place = jnp.where(s < slabs - 1, place, -1)
            inside = (place >= 0) & (place < plane_blocks)
            for n, view in enumerate((opposite, v)):
                target = jnp.where(inside, place - (band_blocks * view - HALO), -1)
                chosen = lax.broadcasted_iota(jnp.int32, (BANDED, count), 0) == target
                chosen = jnp.where(chosen, 1.0, 0.0).astype(jnp.bfloat16)
                total = jnp.dot(chosen, high, preferred_element_type=jnp.float32) + jnp.dot(
                    chosen, low, preferred_element_type=jnp.float32
                )
                if first and index == sets[0]:
                    into[n] = total
                else:
                    into[n] = into[n] + total

    marks = [quads * n // (PIECES - AHEAD + 1) for n in range(PIECES - AHEAD + 2)]
    for n in range(PIECES - AHEAD + 1):
        turn_quads(marks[n], marks[n + 1])
        if n + AHEAD < PIECES:
            for copy in to_x[n + AHEAD]:
                copy.start()
    key_copies[2].wait_recv()
    to_sibling.wait_recv()
    scatter((0, 3), band, True)
    for k in range(2):
        key_copies[k].wait_recv()
        key_copies[3 + k].start()
    for n in range(PIECES):
        for side in range(2):
            to_x[n][side].wait_recv()
            to_fwd[n][side].start()
    scatter((1, 2), band, False)
    for k in range(2):
        key_copies[3 + k].wait_recv()
    for n in range(PIECES):
        for side in range(2):
            to_fwd[n][side].wait_recv()
    scatter((4, 5), band, False)

    for half in range(2):
        lanes = pl.ds(half * LANES, LANES)
        zsend[pl.ds(half, BANDED, stride=2), :] = band[0, :, lanes]
    chunk_rows = [pl.ds(MARKS[c], MARKS[c + 1] - MARKS[c]) for c in range(CHUNKS)]
    to_across = [
        remote(zsend.at[rows], zrecv.at[rows], z_send.at[c], z_recv.at[c], across) for c, rows in enumerate(chunk_rows)
    ]
    for c in range(AHEAD):
        to_across[c].start()
    for half in range(2):
        lanes = pl.ds(half * LANES, LANES)
        plane[1, pl.ds(half, BANDED, stride=2), :] = band[1, :, lanes]
    for c in range(AHEAD, CHUNKS):
        to_across[c - AHEAD].wait_send()
        to_across[c].start()

    lane = lax.broadcasted_iota(jnp.int32, (8, LANES), 1)

    def shift(d, keep, part):
        rows = {}

        def at(c):
            if c not in rows:
                values = plane[d, pl.ds(8 * QUAD * part + c, 8, stride=QUAD), :]
                rows[c] = values if keep is None else values * keep
            return rows[c]

        for i in range(4):
            for q in range(PARTS):
                for dx in range(-3, 4):
                    c, a = divmod(LEAD + NCOL * i + LANES * q + dx, LANES)
                    moved = at(c)
                    if a:
                        moved = pltpu.roll(jnp.where(lane >= a, moved, at(c + 1)), LANES - a, 1)
                    if q == 0 and dx < 0:
                        moved = jnp.where(lane >= -dx, moved, 0.0)
                    if q == PARTS - 1 and dx > 0:
                        moved = jnp.where(lane < NCOL - LANES * q - dx, moved, 0.0)
                    shifted[(d * 7 + dx + 3) * PARTS + q, pl.ds(32 * part + i, 8, stride=4), :] = moved

    def box(planes, t, q):
        sums = [None] * 2
        for d in planes:
            for dx in range(7):
                for dy in range(7):
                    e = d * 49 + dy * 7 + dx
                    weight = weights[e // 8 * PARTS + q, pl.ds(t * 64 + e % 8, 8, stride=8), :]
                    term = weight * shifted[(d * 7 + dx) * PARTS + q, pl.ds(t * 8 + dy, 8), :]
                    n = dx % 2
                    sums[n] = term if sums[n] is None else sums[n] + term
        return sums[0] + sums[1]

    def box_rows(planes, low, high, first):
        @pl.loop(low, high)
        def _(t):
            rows = pl.ds(pl.multiple_of(t * 8, 8), 8)
            for q in range(PARTS):
                total = box(planes, t, q)
                result[q, rows, :] = total if first else result[q, rows, :] + total

    def flatten(part):
        some = min(8, quads - 8 * part)
        pieces = [[] for _ in range(QUAD + 1)]
        for i in range(4):
            for q in range(PARTS):
                values = result[q, pl.ds(32 * part + i, some, stride=4), :]
                c, a = divmod(NCOL * i + LANES * q, LANES)
                end = a + min(LANES, NCOL - LANES * q)
                if a:
                    values = pltpu.roll(values, a, 1)
                pieces[c].append((a, values))
                if end > LANES:
                    pieces[c + 1].append((0, values))
        for c in range(QUAD):
            total = None
            for low, values in sorted(pieces[c], key=lambda piece: piece[0]):
                total = values if total is None else jnp.where(lane[0:some] >= low, values, total)
            out_ref[pl.ds(8 * QUAD * part + c, some, stride=QUAD), 0, :] = total

    to_sides = []
    for c in range(CHUNKS):
        rows = chunk_rows[c]
        to_across[c].wait_recv()
        plane[1, rows, :] = plane[1, rows, :] + zrecv[rows, :]
        to_sides.append(
            [
                remote(plane.at[1, rows], plane.at[target, rows], x_send.at[side, c], x_recv.at[side, c], device)
                for side, (target, device) in enumerate(((0, above), (2, below)))
            ]
        )
        for copy in to_sides[c]:
            copy.start()
        shift(1, None, c)
        box_rows((1,), BOX_MARKS[c], BOX_MARKS[c + 1], True)
    low_keep = (s > 0).astype(jnp.float32)
    high_keep = (s < slabs - 1).astype(jnp.float32)
    for c in range(CHUNKS):
        for copy in to_sides[c]:
            copy.wait_recv()
        shift(0, low_keep, c)
        shift(2, high_keep, c)
        box_rows((0, 2), BOX_MARKS[c], BOX_MARKS[c + 1], False)
        if c:
            flatten(c - 1)
    flatten(CHUNKS - 1)

    for copies in to_x + to_fwd + to_sides + [to_across[CHUNKS - AHEAD :], key_copies, [to_sibling]]:
        for copy in copies:
            copy.wait_send()


def per_device(tiles, lor_weight, block_map, kernel_weight):
    subsets, _, per_dev, lors, width = tiles.shape
    entries, planes, voxels = kernel_weight.shape
    plane_blocks = voxels * lax.axis_size("views") // width
    count = subsets * per_dev
    out_rows = voxels // LANES
    image_rows = voxels // NCOL
    groups = -(-entries // 8)
    hbm = pl.BlockSpec(memory_space=pl.ANY)
    vmem = pl.BlockSpec(memory_space=pltpu.VMEM)
    dma = pltpu.SemaphoreType.DMA
    out = pl.pallas_call(
        functools.partial(kernel, plane_blocks),
        out_shape=jax.ShapeDtypeStruct((out_rows, 1, LANES), jnp.float32),
        in_specs=[hbm, vmem, vmem, hbm],
        out_specs=vmem,
        scratch_shapes=[
            pltpu.VMEM((count * lors, width), jnp.bfloat16),
            pltpu.VMEM((RING, entries, QUAD * LANES), jnp.bfloat16),
            pltpu.VMEM((groups * PARTS, image_rows * 8, LANES), jnp.float32),
            pltpu.VMEM((6, count, width), jnp.float32),
            pltpu.VMEM((6, 8, 384), jnp.int32),
            pltpu.VMEM((2, BANDED, width), jnp.float32),
            pltpu.VMEM((ROWS, LANES), jnp.float32),
            pltpu.VMEM((ROWS, LANES), jnp.float32),
            pltpu.VMEM((3, ROWS + 8, LANES), jnp.float32),
            pltpu.VMEM((21 * PARTS, 128, LANES), jnp.float32),
            pltpu.VMEM((PARTS, 128, LANES), jnp.float32),
            dma((PIECES,)),
            dma((RING,)),
            dma((2, PIECES)),
            dma((2, PIECES)),
            dma((1,)),
            dma((1,)),
            dma((2, PIECES)),
            dma((2, PIECES)),
            dma((5,)),
            dma((5,)),
            dma((CHUNKS,)),
            dma((CHUNKS,)),
            dma((2, CHUNKS)),
            dma((2, CHUNKS)),
        ],
        compiler_params=pltpu.CompilerParams(
            collective_id=0, has_side_effects=True, vmem_limit_bytes=60 * 1024 * 1024
        ),
    )(
        tiles.reshape(count * lors, width),
        jnp.transpose(lor_weight.reshape(subsets, per_dev, lors), (0, 2, 1)),
        block_map.reshape(subsets, 1, per_dev),
        kernel_weight.reshape(entries, voxels),
    )
    return out.reshape(planes, voxels)


def solution(mesh):
    placed = (
        P(None, "slab", "views", None, None),
        P(None, "slab", "views", None),
        P(None, "slab", "views"),
        P(None, "slab", "views"),
    )
    return jax.shard_map(
        per_device, mesh=mesh, in_specs=placed, out_specs=P("slab", "views"), check_vma=False
    )
```

profile of v0, /device:TPU:1, one launch (start us, length us, event | category | flops | bytes accessed | tf_op | source)
XLA Modules:
  0.0 45.5 jit_solution(1819882207792025770)
XLA Ops:
  0.0 43.9 %shard_map.46 = f32[450,1,128]{2,1,0:T(1,128)} custom-call(bf16[5120,256]{1,0:T(8,128)(2,1)} %bitcast.7, bf16[2,16,160]{2,1,0:T(8,128)(2,1)} %bitcast.9, s32[2,1,160]{2,1,0:T(1,128)} %map_ref.1, bf16[147,57600]{1,0:T(8,128)(2,1)} %bitcast.6), custom_call_target="tpu_custom_call" | custom-call | tf_op jit(solution)/shard_map/pallas_call | solution.py:339
  43.9 1.6 %copy.6 = f32[1,57600]{1,0:T(1,128)} copy(f32[1,57600]{1,0:T(1,128)} %bitcast.8) | data formatting | bytes 460800
where the time goes:
time: 45.7 us; the launch traced here: 45.5 us
  Pallas kernels  43.9 us (96%)
  local copies, waits for them, and re-layouts  1.64 us (4%)
    pallas_call x1, Pallas kernels, per_device(): pl.pallas_call(functools.partial(kernel, plane_blocks), out_shape=jax.Sha...  43.9 us
    unnamed x1, local copies, waits for them, and re-layouts  1.64 us

commit v1 on v0

--- a/solution.py
+++ b/solution.py
@@ -22,12 +22,12 @@
 BOX_MARKS = (0, 3, 7, 11, 15)
 PIECES = 4
 AHEAD = 2
-RING = 8
+RING = 4
 
 
 def kernel(
     plane_blocks, tiles_hbm, lor_ref, map_ref, kw_hbm, out_ref,
-    tiles, raw, weights, contrib, keys, band, zsend, zrecv, plane, shifted, result,
+    tiles, raw, stage, weights, contrib, keys, band, zsend, zrecv, plane, shifted, result,
     tile_sem, raw_sem, raw_send, raw_recv, sib_send, sib_recv, fwd_send, fwd_recv, key_send, key_recv,
     z_send, z_recv, x_send, x_recv,
 ):
@@ -37,6 +37,7 @@
     piece = count // PIECES
     band_blocks = voxels // BLOCK
     quads = voxels // (QUAD * LANES)
+    pairs = quads // 2
 
     v = lax.axis_index("views")
     s = lax.axis_index("slab")
@@ -47,14 +48,40 @@
     above = (v, lax.rem(s + 1, slabs))
     below = (v, lax.rem(s + slabs - 1, slabs))
 
+    has_above = s < slabs - 1
+    has_below = s > 0
+
     barrier = pltpu.get_barrier_semaphore()
-    for device in (sibling, across, above, below):
+
+    def greet(device):
         pl.semaphore_signal(barrier, inc=1, device_id=device, device_id_type=MESH)
 
-    def remote(src, dst, send, recv, device):
-        return pltpu.make_async_remote_copy(
-            src_ref=src, dst_ref=dst, send_sem=send, recv_sem=recv, device_id=device, device_id_type=MESH
-        )
+    greet(sibling)
+    greet(across)
+    pl.when(has_above)(lambda: greet(above))
+    pl.when(has_below)(lambda: greet(below))
+
+    class Copy:
+        def __init__(self, src, dst, send, recv, device, there=None, here=None):
+            self.there, self.here = there, here
+            self.copy = pltpu.make_async_remote_copy(
+                src_ref=src, dst_ref=dst, send_sem=send, recv_sem=recv, device_id=device, device_id_type=MESH
+            )
+
+        def on(self, condition, step):
+            if condition is None:
+                step()
+            else:
+                pl.when(condition)(step)
+
+        def start(self):
+            self.on(self.there, self.copy.start)
+
+        def wait_send(self):
+            self.on(self.there, self.copy.wait_send)
+
+        def wait_recv(self):
+            self.on(self.here, self.copy.wait_recv)
 
     piece_rows = piece * lors
     tile_loads = [
@@ -67,36 +94,59 @@
         load.start()
 
     def raw_load(m, slot):
-        lanes = QUAD * LANES
+        lanes = 2 * QUAD * LANES
         start = m * lanes if isinstance(m, int) else pl.multiple_of(m * lanes, lanes)
         return pltpu.make_async_copy(kw_hbm.at[:, pl.ds(start, lanes)], raw.at[slot], raw_sem.at[slot])
 
     for m in range(RING):
         raw_load(m, m).start()
+
+    def sides(for_above, for_below):
+        return ((for_above, above, has_above, has_below), (for_below, below, has_below, has_above))
 
     to_x, to_fwd, key_copies = [], [], []
     for n in range(PIECES):
         rows = pl.ds(n * piece, piece)
         pair = []
-        for side, (target, device) in enumerate(((1, above), (2, below))):
+        for side, (target, device, there, here) in enumerate(sides(1, 2)):
             pair.append(
-                remote(contrib.at[0, rows], contrib.at[target, rows], raw_send.at[side, n], raw_recv.at[side, n], device)
+                Copy(
+                    contrib.at[0, rows], contrib.at[target, rows], raw_send.at[side, n], raw_recv.at[side, n],
+                    device, there, here,
+                )
             )
         to_x.append(pair)
         to_fwd.append(
             [
-                remote(
+                Copy(
                     contrib.at[side + 1, rows], contrib.at[side + 4, rows],
-                    fwd_send.at[side, n], fwd_recv.at[side, n], sibling,
+                    fwd_send.at[side, n], fwd_recv.at[side, n], sibling, has, has,
                 )
-                for side in range(2)
+                for side, has in enumerate((has_below, has_above))
             ]
         )
-    for n, (source, target, device) in enumerate(
-        ((0, 1, above), (0, 2, below), (0, 3, sibling), (1, 4, sibling), (2, 5, sibling))
+    for n, (source, target, device, there, here) in enumerate(
+        (
+            (0, 1, above, has_above, has_below),
+            (0, 2, below, has_below, has_above),
+            (0, 3, sibling, None, None),
+            (1, 4, sibling, has_below, has_below),
+            (2, 5, sibling, has_above, has_above),
+        )
     ):
-        key_copies.append(remote(keys.at[source], keys.at[target], key_send.at[n], key_recv.at[n], device))
-    to_sibling = remote(contrib.at[0], contrib.at[3], sib_send.at[0], sib_recv.at[0], sibling)
+        key_copies.append(
+            Copy(keys.at[source], keys.at[target], key_send.at[n], key_recv.at[n], device, there, here)
+        )
+    to_sibling = Copy(contrib.at[0], contrib.at[3], sib_send.at[0], sib_recv.at[0], sibling)
+
+    def nothing(plane_at, sets):
+        plane[plane_at] = jnp.zeros(plane.shape[1:], jnp.float32)
+        for index in sets:
+            contrib[index] = jnp.zeros(contrib.shape[1:], jnp.float32)
+            keys[index] = jnp.full(keys.shape[1:], -1, jnp.int32)
+
+    pl.when(jnp.logical_not(has_below))(lambda: nothing(0, (1, 4)))
+    pl.when(jnp.logical_not(has_above))(lambda: nothing(2, (2, 5)))
 
     width = keys.shape[2]
     pad = jnp.full((1, width - count), -1, jnp.int32)
@@ -126,7 +176,7 @@
                 preferred_element_type=jnp.float32,
             )
         if n == 0:
-            pl.semaphore_wait(barrier, 4)
+            pl.semaphore_wait(barrier, 2 + has_above.astype(jnp.int32) + has_below.astype(jnp.int32))
             for k in range(3):
                 key_copies[k].start()
         if n < AHEAD:
@@ -139,30 +189,37 @@
     def turn(slot, m):
         for base in range(0, entries, 16):
             size = min(16, entries - base)
-            here = [raw[slot, pl.ds(base, size), pl.ds(c * LANES, LANES)] for c in range(QUAD)]
-            for i in range(4):
-                first, a = divmod(NCOL * i, LANES)
+            for quad in range(2):
+                here = [raw[slot, pl.ds(base, size), pl.ds((quad * QUAD + c) * LANES, LANES)] for c in range(QUAD)]
+                for i in range(4):
+                    first, a = divmod(NCOL * i, LANES)
+                    for q in range(PARTS):
+                        values = here[first + q]
+                        if a:
+                            if first + q + 1 < QUAD:
+                                values = jnp.where(lane16[0:size] >= a, values, here[first + q + 1])
+                            values = pltpu.roll(values, LANES - a, 1)
+                        values = values.astype(jnp.float32)
+                        for half in range(0, size, 8):
+                            some = min(8, size - half)
+                            stage[(base + half) // 8 * PARTS + q, pl.ds((4 * quad + i) * 8, some), :] = values[
+                                half : half + some
+                            ]
+            for e in range(base, base + size):
                 for q in range(PARTS):
-                    values = here[first + q]
-                    if a:
-                        if first + q + 1 < QUAD:
-                            values = jnp.where(lane16[0:size] >= a, values, here[first + q + 1])
-                        values = pltpu.roll(values, LANES - a, 1)
-                    values = values.astype(jnp.float32)
-                    for half in range(0, size, 8):
-                        some = min(8, size - half)
-                        weights[(base + half) // 8 * PARTS + q, pl.ds((4 * m + i) * 8, some), :] = values[
-                            half : half + some
-                        ]
-
-    def turn_quads(low, high):
+                    block = e // 8 * PARTS + q
+                    weights[block, pl.ds(pl.multiple_of(m * 64 + e % 8 * 8, 8), 8), :] = stage[
+                        block, pl.ds(e % 8, 8, stride=8), :
+                    ]
+
+    def turn_pairs(low, high):
         @pl.loop(low, high)
         def _(m):
             slot = lax.rem(m, RING)
             raw_load(m, slot).wait()
             turn(slot, m)
 
-            @pl.when(m + RING < quads)
+            @pl.when(m + RING < pairs)
             def _():
                 raw_load(m + RING, slot).start()
 
@@ -173,10 +230,6 @@
             high = whole.astype(jnp.bfloat16)
             low = (whole - high.astype(jnp.float32)).astype(jnp.bfloat16)
             place = keys[index][0:1, 0:count] - plane_blocks * (1 - delta)
-            if delta < 0:
-                place = jnp.where(s > 0, place, -1)
-            if delta > 0:
-                place = jnp.where(s < slabs - 1, place, -1)
             inside = (place >= 0) & (place < plane_blocks)
             for n, view in enumerate((opposite, v)):
                 target = jnp.where(inside, place - (band_blocks * view - HALO), -1)
@@ -190,23 +243,26 @@
                 else:
                     into[n] = into[n] + total
 
-    marks = [quads * n // (PIECES - AHEAD + 1) for n in range(PIECES - AHEAD + 2)]
-    for n in range(PIECES - AHEAD + 1):
-        turn_quads(marks[n], marks[n + 1])
-        if n + AHEAD < PIECES:
-            for copy in to_x[n + AHEAD]:
-                copy.start()
-    key_copies[2].wait_recv()
-    to_sibling.wait_recv()
-    scatter((0, 3), band, True)
+    turn_pairs(0, pairs // 3)
+    for n in range(AHEAD, PIECES):
+        for copy in to_x[n]:
+            copy.start()
+    turn_pairs(pairs // 3, pairs * 2 // 3)
     for k in range(2):
         key_copies[k].wait_recv()
         key_copies[3 + k].start()
-    for n in range(PIECES):
+    for n in range(AHEAD):
         for side in range(2):
             to_x[n][side].wait_recv()
             to_fwd[n][side].start()
-    scatter((1, 2), band, False)
+    turn_pairs(pairs * 2 // 3, pairs)
+    for n in range(AHEAD, PIECES):
+        for side in range(2):
+            to_x[n][side].wait_recv()
+            to_fwd[n][side].start()
+    key_copies[2].wait_recv()
+    to_sibling.wait_recv()
+    scatter((0, 3, 1, 2), band, True)
     for k in range(2):
         key_copies[3 + k].wait_recv()
     for n in range(PIECES):
@@ -219,7 +275,7 @@
         zsend[pl.ds(half, BANDED, stride=2), :] = band[0, :, lanes]
     chunk_rows = [pl.ds(MARKS[c], MARKS[c + 1] - MARKS[c]) for c in range(CHUNKS)]
     to_across = [
-        remote(zsend.at[rows], zrecv.at[rows], z_send.at[c], z_recv.at[c], across) for c, rows in enumerate(chunk_rows)
+        Copy(zsend.at[rows], zrecv.at[rows], z_send.at[c], z_recv.at[c], across) for c, rows in enumerate(chunk_rows)
     ]
     for c in range(AHEAD):
         to_across[c].start()
@@ -232,13 +288,12 @@
 
     lane = lax.broadcasted_iota(jnp.int32, (8, LANES), 1)
 
-    def shift(d, keep, part):
+    def shift(d, part):
         rows = {}
 
         def at(c):
             if c not in rows:
-                values = plane[d, pl.ds(8 * QUAD * part + c, 8, stride=QUAD), :]
-                rows[c] = values if keep is None else values * keep
+                rows[c] = plane[d, pl.ds(8 * QUAD * part + c, 8, stride=QUAD), :]
             return rows[c]
 
         for i in range(4):
@@ -260,7 +315,7 @@
             for dx in range(7):
                 for dy in range(7):
                     e = d * 49 + dy * 7 + dx
-                    weight = weights[e // 8 * PARTS + q, pl.ds(t * 64 + e % 8, 8, stride=8), :]
+                    weight = weights[e // 8 * PARTS + q, pl.ds(pl.multiple_of(t * 64 + e % 8 * 8, 8), 8), :]
                     term = weight * shifted[(d * 7 + dx) * PARTS + q, pl.ds(t * 8 + dy, 8), :]
                     n = dx % 2
                     sums[n] = term if sums[n] is None else sums[n] + term
@@ -300,21 +355,22 @@
         plane[1, rows, :] = plane[1, rows, :] + zrecv[rows, :]
         to_sides.append(
             [
-                remote(plane.at[1, rows], plane.at[target, rows], x_send.at[side, c], x_recv.at[side, c], device)
-                for side, (target, device) in enumerate(((0, above), (2, below)))
+                Copy(
+                    plane.at[1, rows], plane.at[target, rows], x_send.at[side, c], x_recv.at[side, c],
+                    device, there, here,
+                )
+                for side, (target, device, there, here) in enumerate(sides(0, 2))
             ]
         )
         for copy in to_sides[c]:
             copy.start()
-        shift(1, None, c)
+        shift(1, c)
         box_rows((1,), BOX_MARKS[c], BOX_MARKS[c + 1], True)
-    low_keep = (s > 0).astype(jnp.float32)
-    high_keep = (s < slabs - 1).astype(jnp.float32)
     for c in range(CHUNKS):
         for copy in to_sides[c]:
             copy.wait_recv()
-        shift(0, low_keep, c)
-        shift(2, high_keep, c)
+        shift(0, c)
+        shift(2, c)
         box_rows((0, 2), BOX_MARKS[c], BOX_MARKS[c + 1], False)
         if c:
             flatten(c - 1)
@@ -343,7 +399,8 @@
         out_specs=vmem,
         scratch_shapes=[
             pltpu.VMEM((count * lors, width), jnp.bfloat16),
-            pltpu.VMEM((RING, entries, QUAD * LANES), jnp.bfloat16),
+            pltpu.VMEM((RING, entries, 2 * QUAD * LANES), jnp.bfloat16),
+            pltpu.VMEM((groups * PARTS, 64, LANES), jnp.float32),
             pltpu.VMEM((groups * PARTS, image_rows * 8, LANES), jnp.float32),
             pltpu.VMEM((6, count, width), jnp.float32),
             pltpu.VMEM((6, 8, 384), jnp.int32),

time: 45.7 us -> 40.3 us (0.88)
  the two profiles are of different devices: /device:TPU:1 before, /device:TPU:32 now
where the time goes in v1:
time: 40.3 us; the launch traced here: 40.1 us
  Pallas kernels  38.4 us (95%)
  local copies, waits for them, and re-layouts  1.64 us (4%)
    pallas_call x1, Pallas kernels, per_device(): pl.pallas_call(functools.partial(kernel, plane_blocks), out_shape=jax.Sha...  38.4 us
    unnamed x1, local copies, waits for them, and re-layouts  1.64 us

profile of v1, /device:TPU:32, one launch (start us, length us, event | category | flops | bytes accessed | tf_op | source)
XLA Modules:
  0.0 40.1 jit_solution(12189574576579409584)
XLA Ops:
  0.0 38.4 %shard_map.46 = f32[450,1,128]{2,1,0:T(1,128)} custom-call(bf16[5120,256]{1,0:T(8,128)(2,1)} %bitcast.7, bf16[2,16,160]{2,1,0:T(8,128)(2,1)} %bitcast.9, s32[2,1,160]{2,1,0:T(1,128)} %map_ref.1, bf16[147,57600]{1,0:T(8,128)(2,1)} %bitcast.6), custom_call_target="tpu_custom_call" | custom-call | tf_op jit(solution)/shard_map/pallas_call | solution.py:395
  38.4 1.6 %copy.6 = f32[1,57600]{1,0:T(1,128)} copy(f32[1,57600]{1,0:T(1,128)} %bitcast.8) | data formatting | bytes 460800

commit v2 on v1

--- a/solution.py
+++ b/solution.py
@@ -182,8 +182,6 @@
         if n < AHEAD:
             for copy in to_x[n]:
                 copy.start()
-    to_sibling.start()
-
     lane16 = lax.broadcasted_iota(jnp.int32, (16, LANES), 1)
 
     def turn(slot, m):
@@ -205,12 +203,13 @@
                             stage[(base + half) // 8 * PARTS + q, pl.ds((4 * quad + i) * 8, some), :] = values[
                                 half : half + some
                             ]
-            for e in range(base, base + size):
+            for e in range(base, base + size, 2):
                 for q in range(PARTS):
                     block = e // 8 * PARTS + q
-                    weights[block, pl.ds(pl.multiple_of(m * 64 + e % 8 * 8, 8), 8), :] = stage[
-                        block, pl.ds(e % 8, 8, stride=8), :
-                    ]
+                    both = [stage[block, pl.ds(min(e + n, entries - 1) % 8, 8, stride=8), :] for n in range(2)]
+                    weights[block, pl.ds(pl.multiple_of(m * 64 + e % 8 * 8, 16), 16), :] = jnp.concatenate(
+                        both, axis=0
+                    ).astype(jnp.bfloat16)
 
     def turn_pairs(low, high):
         @pl.loop(low, high)
@@ -247,6 +246,7 @@
     for n in range(AHEAD, PIECES):
         for copy in to_x[n]:
             copy.start()
+    to_sibling.start()
     turn_pairs(pairs // 3, pairs * 2 // 3)
     for k in range(2):
         key_copies[k].wait_recv()
@@ -311,14 +311,18 @@
 
     def box(planes, t, q):
         sums = [None] * 2
-        for d in planes:
-            for dx in range(7):
-                for dy in range(7):
-                    e = d * 49 + dy * 7 + dx
-                    weight = weights[e // 8 * PARTS + q, pl.ds(pl.multiple_of(t * 64 + e % 8 * 8, 8), 8), :]
-                    term = weight * shifted[(d * 7 + dx) * PARTS + q, pl.ds(t * 8 + dy, 8), :]
-                    n = dx % 2
-                    sums[n] = term if sums[n] is None else sums[n] + term
+        for pair in range(0, entries, 2):
+            wanted = [e for e in (pair, pair + 1) if e < entries and e // 49 in planes]
+            if not wanted:
+                continue
+            both = weights[
+                pair // 8 * PARTS + q, pl.ds(pl.multiple_of(t * 64 + pair % 8 * 8, 16), 16), :
+            ].astype(jnp.float32)
+            for e in wanted:
+                d, dy, dx = e // 49, e // 7 % 7, e % 7
+                n = e % 2
+                term = both[8 * n : 8 * n + 8] * shifted[(d * 7 + dx) * PARTS + q, pl.ds(t * 8 + dy, 8), :]
+                sums[n] = term if sums[n] is None else sums[n] + term
         return sums[0] + sums[1]
 
     def box_rows(planes, low, high, first):
@@ -401,7 +405,7 @@
             pltpu.VMEM((count * lors, width), jnp.bfloat16),
             pltpu.VMEM((RING, entries, 2 * QUAD * LANES), jnp.bfloat16),
             pltpu.VMEM((groups * PARTS, 64, LANES), jnp.float32),
-            pltpu.VMEM((groups * PARTS, image_rows * 8, LANES), jnp.float32),
+            pltpu.VMEM((groups * PARTS, image_rows * 8, LANES), jnp.bfloat16),
             pltpu.VMEM((6, count, width), jnp.float32),
             pltpu.VMEM((6, 8, 384), jnp.int32),
             pltpu.VMEM((2, BANDED, width), jnp.float32),

time: 40.3 us -> 40.1 us (level)
  no operation moved by 1% of the time
where the time goes in v2:
time: 40.1 us; the launch traced here: 39.9 us
  Pallas kernels  38.3 us (96%)
  local copies, waits for them, and re-layouts  1.64 us (4%)
    pallas_call x1, Pallas kernels, per_device(): pl.pallas_call(functools.partial(kernel, plane_blocks), out_shape=jax.Sha...  38.3 us
    unnamed x1, local copies, waits for them, and re-layouts  1.64 us

profile of v2, /device:TPU:32, one launch (start us, length us, event | category | flops | bytes accessed | tf_op | source)
XLA Modules:
  0.0 39.9 jit_solution(3113746633481759819)
XLA Ops:
  0.0 38.3 %shard_map.46 = f32[450,1,128]{2,1,0:T(1,128)} custom-call(bf16[5120,256]{1,0:T(8,128)(2,1)} %bitcast.7, bf16[2,16,160]{2,1,0:T(8,128)(2,1)} %bitcast.9, s32[2,1,160]{2,1,0:T(1,128)} %map_ref.1, bf16[147,57600]{1,0:T(8,128)(2,1)} %bitcast.6), custom_call_target="tpu_custom_call" | custom-call | tf_op jit(solution)/shard_map/pallas_call | solution.py:399
  38.3 1.6 %copy.6 = f32[1,57600]{1,0:T(1,128)} copy(f32[1,57600]{1,0:T(1,128)} %bitcast.8) | data formatting | bytes 460800

commit v3 on v2

--- a/solution.py
+++ b/solution.py
@@ -103,6 +103,10 @@
 
     def sides(for_above, for_below):
         return ((for_above, above, has_above, has_below), (for_below, below, has_below, has_above))
+
+    def begin(pair):
+        for copy in pair:
+            copy.start()
 
     to_x, to_fwd, key_copies = [], [], []
     for n in range(PIECES):
@@ -179,9 +183,7 @@
             pl.semaphore_wait(barrier, 2 + has_above.astype(jnp.int32) + has_below.astype(jnp.int32))
             for k in range(3):
                 key_copies[k].start()
-        if n < AHEAD:
-            for copy in to_x[n]:
-                copy.start()
+        begin(to_x[n])
     lane16 = lax.broadcasted_iota(jnp.int32, (16, LANES), 1)
 
     def turn(slot, m):
@@ -222,17 +224,17 @@
             def _():
                 raw_load(m + RING, slot).start()
 
-    def scatter(sets, into, first):
+    def scatter(sets, into, first, start, stop):
         for index in sets:
             delta = (0, -1, 1)[index % 3]
-            whole = contrib[index]
+            whole = contrib[index, start:stop, :]
             high = whole.astype(jnp.bfloat16)
             low = (whole - high.astype(jnp.float32)).astype(jnp.bfloat16)
-            place = keys[index][0:1, 0:count] - plane_blocks * (1 - delta)
+            place = keys[index][0:1, start:stop] - plane_blocks * (1 - delta)
             inside = (place >= 0) & (place < plane_blocks)
             for n, view in enumerate((opposite, v)):
                 target = jnp.where(inside, place - (band_blocks * view - HALO), -1)
-                chosen = lax.broadcasted_iota(jnp.int32, (BANDED, count), 0) == target
+                chosen = lax.broadcasted_iota(jnp.int32, (BANDED, stop - start), 0) == target
                 chosen = jnp.where(chosen, 1.0, 0.0).astype(jnp.bfloat16)
                 total = jnp.dot(chosen, high, preferred_element_type=jnp.float32) + jnp.dot(
                     chosen, low, preferred_element_type=jnp.float32
@@ -242,12 +244,8 @@
                 else:
                     into[n] = into[n] + total
 
-    turn_pairs(0, pairs // 3)
-    for n in range(AHEAD, PIECES):
-        for copy in to_x[n]:
-            copy.start()
     to_sibling.start()
-    turn_pairs(pairs // 3, pairs * 2 // 3)
+    turn_pairs(0, pairs)
     for k in range(2):
         key_copies[k].wait_recv()
         key_copies[3 + k].start()
@@ -255,20 +253,21 @@
         for side in range(2):
             to_x[n][side].wait_recv()
             to_fwd[n][side].start()
-    turn_pairs(pairs * 2 // 3, pairs)
     for n in range(AHEAD, PIECES):
         for side in range(2):
             to_x[n][side].wait_recv()
             to_fwd[n][side].start()
     key_copies[2].wait_recv()
     to_sibling.wait_recv()
-    scatter((0, 3, 1, 2), band, True)
+    scatter((0, 3, 1, 2), band, True, 0, count)
     for k in range(2):
         key_copies[3 + k].wait_recv()
     for n in range(PIECES):
         for side in range(2):
             to_fwd[n][side].wait_recv()
-    scatter((4, 5), band, False)
+        if n == PIECES - 2:
+            scatter((4, 5), band, False, 0, count - piece)
+    scatter((4, 5), band, False, count - piece, count)
 
     for half in range(2):
         lanes = pl.ds(half * LANES, LANES)
@@ -366,8 +365,7 @@
                 for side, (target, device, there, here) in enumerate(sides(0, 2))
             ]
         )
-        for copy in to_sides[c]:
-            copy.start()
+        begin(to_sides[c])
         shift(1, c)
         box_rows((1,), BOX_MARKS[c], BOX_MARKS[c + 1], True)
     for c in range(CHUNKS):

time: 40.1 us -> 40 us (level)
  no operation moved by 1% of the time
where the time goes in v3:
time: 40 us; the launch traced here: 39.8 us
  Pallas kernels  38.2 us (96%)
  local copies, waits for them, and re-layouts  1.64 us (4%)
    pallas_call x1, Pallas kernels, per_device(): pl.pallas_call(functools.partial(kernel, plane_blocks), out_shape=jax.Sha...  38.2 us
    unnamed x1, local copies, waits for them, and re-layouts  1.64 us

profile of v3, /device:TPU:32, one launch (start us, length us, event | category | flops | bytes accessed | tf_op | source)
XLA Modules:
  0.0 39.8 jit_solution(7185002113165314893)
XLA Ops:
  0.0 38.2 %shard_map.46 = f32[450,1,128]{2,1,0:T(1,128)} custom-call(bf16[5120,256]{1,0:T(8,128)(2,1)} %bitcast.7, bf16[2,16,160]{2,1,0:T(8,128)(2,1)} %bitcast.9, s32[2,1,160]{2,1,0:T(1,128)} %map_ref.1, bf16[147,57600]{1,0:T(8,128)(2,1)} %bitcast.6), custom_call_target="tpu_custom_call" | custom-call | tf_op jit(solution)/shard_map/pallas_call | solution.py:397
  38.2 1.6 %copy.6 = f32[1,57600]{1,0:T(1,128)} copy(f32[1,57600]{1,0:T(1,128)} %bitcast.8) | data formatting | bytes 460800
